TPU v7x, 32 devices: a whole 2x2x4 slice. The times are simulated.
32 devices in a mesh: groups: 2 (over x), row: 2 (over core), col: 8 (over z, y).
Axes of the slice: x: 2, y: 2, z: 4, core: 2. Of those that a mesh axis runs over, the one named last changes fastest.
Arguments:
- payload: bfloat16 [2, 768, 3584], P(None, ('groups', 'row', 'col')), parts along dimension 1, may hold values from -448 to 448
- block_scales: bfloat16 [2, 768, 28], P(None, ('groups', 'row', 'col')), parts along dimension 1, may hold values from 0.0049743652 to 0.049804688
- expert_ids: int32 [2, 768, 8], P(None, ('groups', 'row', 'col')), parts along dimension 1, may hold values from 0 to 15, all different within a row; in each aligned block of 24 rows (0 to 23, 24 to 47, ..., all dimensions but the last counted through in order) at most 12 rows name the same one
- gate_codes: int32 [2, 768, 8], P(None, ('groups', 'row', 'col')), parts along dimension 1, may hold values from 1 to 255
- w_gate: bfloat16 [16, 3584, 1024], P(('row', 'col')), may hold values from -0.09375 to 0.09375
- w_up: bfloat16 [16, 3584, 1024], P(('row', 'col')), may hold values from -0.09375 to 0.09375
- w_down: bfloat16 [16, 1024, 3584], P(('row', 'col')), may hold values from -0.1875 to 0.1875
Outputs:
- mixed: bfloat16 [2, 768, 3584], P(None, ('groups', 'row', 'col')), parts along dimension 1
There are 2 independent parts, one for each index of `groups`. A program takes and returns all parts, laid end to end along the dimension named above; an argument that names none is the same for every part. Nothing has to cross between parts.
Inputs may be any that keep to these rules, and one draw needn't show every extreme that they name: `expert_ids`: each token names 8 different experts; in each micro-batch the 24 tokens of one device name no expert more than 12 times, a bound that some block reaches.
All inputs are finite; a program needn't handle non-finite values.
Results may differ from a plain program's by a relative error of at most 0.008.
Values may be sent and summed in bfloat16 or wider, within the bound.
A program may use at most 128 MiB of HBM per device.

v0:
```python
import jax
import jax.numpy as jnp
from jax import lax
from jax.sharding import PartitionSpec as P


def dequantize(values, block_scales):
    shaped = values.astype(jnp.float32).reshape(values.shape[:-1] + (block_scales.shape[-1], 128))
    scaled = shaped * block_scales.astype(jnp.float32)[..., None]
    return scaled.reshape(values.shape).astype(jnp.bfloat16)


def expert_rows(inputs, gate_matrix, up_matrix, down_matrix):
    gate = jnp.dot(inputs, gate_matrix, preferred_element_type=jnp.float32)
    upward = jnp.dot(inputs, up_matrix, preferred_element_type=jnp.float32)
    hidden = (jax.nn.silu(gate) * upward).astype(jnp.bfloat16)
    return jnp.dot(hidden, down_matrix, preferred_element_type=jnp.float32).astype(jnp.bfloat16)


def block_slots(choices, expert_count):
    catalog = jnp.arange(expert_count, dtype=jnp.int32)
    named = (choices[..., None] == catalog).astype(jnp.int32)
    per_token = jnp.sum(named, axis=-2)
    before = jnp.cumsum(per_token, axis=-2) - per_token
    return jnp.sum(named * before[..., None, :], axis=-1)


def token_weights(codes):
    values = codes.astype(jnp.float32)
    return values / jnp.sum(values, axis=-1, keepdims=True)


def shards(payload, block_scales, expert_ids, gate_codes, w_gate, w_up, w_down):
    width = payload.shape[2]
    scale_count = block_scales.shape[2]
    n_row = lax.axis_size("row")
    n_col = lax.axis_size("col")
    results = []
    for batch_index in range(payload.shape[0]):
        choices = expert_ids[batch_index : batch_index + 1]
        batches, tokens_here, picks = choices.shape
        capacity = tokens_here // 2
        slots = block_slots(choices, n_row * n_col)
        micro_ids = jnp.arange(batches, dtype=jnp.int32)[:, None, None]
        position = ((choices * batches + micro_ids) * capacity + slots).reshape(-1)
        slot_total = n_row * n_col * batches * capacity
        spread_rows = jnp.broadcast_to(
            payload[batch_index : batch_index + 1][:, :, None, :],
            (batches, tokens_here, picks, width),
        ).reshape(-1, width)
        spread_scales = jnp.broadcast_to(
            block_scales[batch_index : batch_index + 1][:, :, None, :],
            (batches, tokens_here, picks, scale_count),
        ).reshape(-1, scale_count)
        send_rows = jnp.zeros((slot_total, width), jnp.bfloat16).at[position].set(spread_rows)
        send_scales = (
            jnp.zeros((slot_total, scale_count), jnp.bfloat16).at[position].set(spread_scales)
        )
        send_rows = send_rows.reshape(n_row * n_col, batches * capacity, width)
        send_scales = send_scales.reshape(n_row * n_col, batches * capacity, scale_count)
        arrived = lax.all_to_all(send_rows, ("row", "col"), split_axis=0, concat_axis=0, tiled=True)
        arrived_scales = lax.all_to_all(
            send_scales, ("row", "col"), split_axis=0, concat_axis=0, tiled=True
        )
        dequant = dequantize(arrived, arrived_scales)
        outer = dequant.shape[0]
        inner = dequant.shape[1]
        result = expert_rows(dequant.reshape(outer * inner, width), w_gate[0], w_up[0], w_down[0])
        outputs = result.reshape(outer, inner, width)
        returned = lax.all_to_all(outputs, ("row", "col"), split_axis=0, concat_axis=0, tiled=True)
        picked = returned.reshape(-1, width)[position].reshape(batches, tokens_here, picks, width)
        results.append(
            jnp.einsum(
                "mbk,mbkd->mbd",
                token_weights(gate_codes[batch_index : batch_index + 1]),
                picked.astype(jnp.float32),
            )
        )
    totals = jnp.concatenate(results, axis=0)
    return totals.astype(jnp.bfloat16)


def solution(mesh):
    placed = (
        P(None, ("groups", "row", "col"), None),
        P(None, ("groups", "row", "col"), None),
        P(None, ("groups", "row", "col"), None),
        P(None, ("groups", "row", "col"), None),
        P(("row", "col"), None, None),
        P(("row", "col"), None, None),
        P(("row", "col"), None, None),
    )
    return jax.shard_map(
        shards,
        mesh=mesh,
        in_specs=placed,
        out_specs=P(None, ("groups", "row", "col"), None),
        check_vma=False,
    )
```

profile of v0, /device:TPU:0, one launch (start us, length us, event | category | flops | bytes accessed | tf_op | source)
XLA Modules:
  0.0 221.1 jit_solution(12893132638010508433)
XLA Ops:
  0.0 0.7 slice_bitcast_fusion.5
  0.7 0.1 copy.42
  0.8 0.1 copy.44
  0.9 0.7 bitcast_add_fusion.1
  1.7 0.1 copy.48
  1.8 0.1 copy.50
  1.9 0.7 bitcast_add_fusion
  2.6 0.1 copy.51
  2.7 0.1 reshape.233
  2.8 0.7 slice_bitcast_fusion.3
  3.5 1.0 scatter_custom_fusion.3
  4.5 0.7 reshape.300
  5.3 7.4 %all-to-all-start.4 = ((bf16[16,2,168]{2,1,0:T(2,128)(2,1)}), bf16[16,2,168]{2,1,0:T(2,128)(2,1)S(1)}, u32[]{:S(2)}, u32[]{:S(2)}) async-start(bf16[16,2,168]{2,1,0:T(2,128)(2,1)} %reshape.300), calls=%async_computation.4 | async-start | bytes 32768 | tf_op jit(solution)/shard_map/all_to_all | solution.py:62
  12.7 0.1 copy.45
  12.7 0.1 reshape.225
  12.8 1.0 scatter_custom_fusion.1
  13.9 0.7 reshape.302
  14.6 4.5 %all-to-all-done.4 = bf16[16,2,168]{2,1,0:T(2,128)(2,1)S(1)} async-done(((bf16[16,2,168]{2,1,0:T(2,128)(2,1)}), bf16[16,2,168]{2,1,0:T(2,128)(2,1)S(1)}, u32[]{:S(2)}, u32[]{:S(2)}) %all-to-all-start.4) | async-done | bytes 10784 | tf_op jit(solution)/shard_map/all_to_all | solution.py:62
  19.1 3.5 %all-to-all-start.1 = ((bf16[16,2,168]{2,1,0:T(2,128)(2,1)}), bf16[16,2,168]{2,1,0:T(2,128)(2,1)S(1)}, u32[]{:S(2)}, u32[]{:S(2)}) async-start(bf16[16,2,168]{2,1,0:T(2,128)(2,1)} %reshape.302), calls=%async_computation.1 | async-start | bytes 32768 | tf_op jit(solution)/shard_map/all_to_all | solution.py:62
  22.6 1.0 slice_bitcast_fusion.1
  23.6 2.9 %scatter_custom_fusion.2 = bf16[192,3584]{1,0:T(8,128)(2,1)S(1)} fusion(s32[192]{0:T(256)S(1)} %bitcast.96, bf16[24,3584]{1,0:T(8,128)(2,1)S(1)} %get-tuple-element.8, bf16[]{:T(256)} %constant.9.clone.1), kind=kCustom, calls=%fused_computation.26 | custom fusion | bytes 1548290 | tf_op jit(solution)/shard_map/scatter | solution.py:55
  26.5 1.5 reshape.234
  28.0 1.0 all-to-all-done.1
  29.0 5.0 %all-to-all-start.3 = ((bf16[16,12,3584]{2,1,0:T(8,128)(2,1)}), bf16[16,12,3584]{2,1,0:T(8,128)(2,1)}, u32[]{:S(2)}, u32[]{:S(2)}) async-start(bf16[16,12,3584]{2,1,0:T(8,128)(2,1)} %reshape.234), calls=%async_computation.3 | async-start | bytes 3670016 | tf_op jit(solution)/shard_map/all_to_all | solution.py:61
  34.0 2.9 %scatter_custom_fusion = bf16[192,3584]{1,0:T(8,128)(2,1)S(1)} fusion(s32[192]{0:T(256)S(1)} %bitcast.99, bf16[24,3584]{1,0:T(8,128)(2,1)S(1)} %get-tuple-element.7, bf16[]{:T(256)} %constant.9.clone.1), kind=kCustom, calls=%fused_computation.30 | custom fusion | bytes 1548290 | tf_op jit(solution)/shard_map/scatter | solution.py:55
  36.8 1.5 reshape.226
  38.3 0.1 reshape.301
  38.5 0.9 mul.68
  39.3 1.8 mul.69
  41.2 0.1 reshape.303
  41.3 0.9 mul.60
  42.2 1.8 mul.61
  44.0 32.3 %all-to-all-done.3 = bf16[16,12,3584]{2,1,0:T(8,128)(2,1)} async-done(((bf16[16,12,3584]{2,1,0:T(8,128)(2,1)}), bf16[16,12,3584]{2,1,0:T(8,128)(2,1)}, u32[]{:S(2)}, u32[]{:S(2)}) %all-to-all-start.3) | async-done | bytes 1376288 | tf_op jit(solution)/shard_map/all_to_all | solution.py:61
  76.3 4.8 %all-to-all-start = ((bf16[16,12,3584]{2,1,0:T(8,128)(2,1)}), bf16[16,12,3584]{2,1,0:T(8,128)(2,1)}, u32[]{:S(2)}, u32[]{:S(2)}) async-start(bf16[16,12,3584]{2,1,0:T(8,128)(2,1)} %reshape.226), calls=%async_computation | async-start | bytes 3670016 | tf_op jit(solution)/shard_map/all_to_all | solution.py:61
  81.1 0.0 copy-done.1
  81.2 4.3 %fusion.18 = bf16[16,12,3584]{2,1,0:T(8,128)(2,1)} fusion(f32[16,12,3584]{2,0,1:T(8,128)S(1)} %copy-done.1, bf16[16,12,3584]{2,1,0:T(8,128)(2,1)} %all-to-all-done.3), kind=kLoop, calls=%fused_computation.21 | loop fusion | flops 2064384 | bytes 5505024 | tf_op jit(solution)/shard_map/convert_element_type | solution.py:10
  85.5 2.4 %reshape.236 = bf16[192,3584]{1,0:T(8,128)(2,1)S(1)} reshape(bf16[16,12,3584]{2,1,0:T(8,128)(2,1)} %fusion.18) | data formatting | bytes 2752512 | tf_op jit(solution)/shard_map/reshape | solution.py:68
  87.8 5.6 %fusion.8 = f32[192,1024]{1,0:T(8,128)} fusion(bf16[192,3584]{1,0:T(8,128)(2,1)S(1)} %reshape.236, bf16[1,3584,1024]{2,1,0:T(8,128)(2,1)} %param.11), kind=kOutput, calls=%fused_computation.14 | convolution fusion | flops 1409286144 | bytes 9502720 | tf_op jit(solution)/shard_map/dot_general | solution.py:14
  93.4 8.5 %fusion.15 = bf16[192,3584]{1,0:T(8,128)(2,1)S(1)} fusion(bf16[1,1024,3584]{2,1,0:T(8,128)(2,1)} %param.13, bf16[192,3584]{1,0:T(8,128)(2,1)S(1)} %reshape.236, bf16[1,3584,1024]{2,1,0:T(8,128)(2,1)} %param.12, f32[192,1024]{1,0:T(8,128)} %fusion.8), kind=kOutput, calls=%fused_computation.19 | convolution fusion | flops 2820440064 | bytes 18219008 | tf_op jit(solution)/shard_map/dot_general | solution.py:17
  101.9 1.4 reshape.237
  103.3 20.2 %all-to-all-done = bf16[16,12,3584]{2,1,0:T(8,128)(2,1)} async-done(((bf16[16,12,3584]{2,1,0:T(8,128)(2,1)}), bf16[16,12,3584]{2,1,0:T(8,128)(2,1)}, u32[]{:S(2)}, u32[]{:S(2)}) %all-to-all-start) | async-done | bytes 1376288 | tf_op jit(solution)/shard_map/all_to_all | solution.py:61
  123.5 4.8 %all-to-all-start.5 = ((bf16[16,12,3584]{2,1,0:T(8,128)(2,1)}), bf16[16,12,3584]{2,1,0:T(8,128)(2,1)}, u32[]{:S(2)}, u32[]{:S(2)}) async-start(bf16[16,12,3584]{2,1,0:T(8,128)(2,1)} %reshape.237), calls=%async_computation.5 | async-start | bytes 3670016 | tf_op jit(solution)/shard_map/all_to_all | solution.py:70
  128.3 0.0 copy-done
  128.3 4.4 %fusion.19 = bf16[16,12,3584]{2,1,0:T(8,128)(2,1)} fusion(f32[16,12,3584]{2,0,1:T(8,128)S(1)} %copy-done, bf16[16,12,3584]{2,1,0:T(8,128)(2,1)} %all-to-all-done), kind=kLoop, calls=%fused_computation.23 | loop fusion | flops 2064384 | bytes 5505024 | tf_op jit(solution)/shard_map/convert_element_type | solution.py:10
  132.7 2.4 %reshape.228 = bf16[192,3584]{1,0:T(8,128)(2,1)S(1)} reshape(bf16[16,12,3584]{2,1,0:T(8,128)(2,1)} %fusion.19) | data formatting | bytes 2752512 | tf_op jit(solution)/shard_map/reshape | solution.py:68
  135.1 5.6 %fusion.10 = f32[192,1024]{1,0:T(8,128)} fusion(bf16[192,3584]{1,0:T(8,128)(2,1)S(1)} %reshape.228, bf16[1,3584,1024]{2,1,0:T(8,128)(2,1)} %param.11), kind=kOutput, calls=%fused_computation.16 | convolution fusion | flops 1409286144 | bytes 9502720 | tf_op jit(solution)/shard_map/dot_general | solution.py:14
  140.6 8.5 %fusion.12 = bf16[192,3584]{1,0:T(8,128)(2,1)S(1)} fusion(bf16[1,1024,3584]{2,1,0:T(8,128)(2,1)} %param.13, bf16[192,3584]{1,0:T(8,128)(2,1)S(1)} %reshape.228, bf16[1,3584,1024]{2,1,0:T(8,128)(2,1)} %param.12, f32[192,1024]{1,0:T(8,128)} %fusion.10), kind=kOutput, calls=%fused_computation.18 | convolution fusion | flops 2820440064 | bytes 18219008 | tf_op jit(solution)/shard_map/dot_general | solution.py:17
  149.1 1.4 reshape.229
  150.6 20.1 %all-to-all-done.5 = bf16[16,12,3584]{2,1,0:T(8,128)(2,1)} async-done(((bf16[16,12,3584]{2,1,0:T(8,128)(2,1)}), bf16[16,12,3584]{2,1,0:T(8,128)(2,1)}, u32[]{:S(2)}, u32[]{:S(2)}) %all-to-all-start.5) | async-done | bytes 1376288 | tf_op jit(solution)/shard_map/all_to_all | solution.py:70
  170.7 4.8 %all-to-all-start.2 = ((bf16[16,12,3584]{2,1,0:T(8,128)(2,1)}), bf16[16,12,3584]{2,1,0:T(8,128)(2,1)S(1)}, u32[]{:S(2)}, u32[]{:S(2)}) async-start(bf16[16,12,3584]{2,1,0:T(8,128)(2,1)} %reshape.229), calls=%async_computation.2 | async-start | bytes 3670016 | tf_op jit(solution)/shard_map/all_to_all | solution.py:70
  175.4 0.0 copy-done.3
  175.5 0.7 copy.56
  176.2 0.7 copy.54
  176.9 0.6 pad_clamp_fusion.1
  177.4 2.4 %reshape.238 = bf16[192,3584]{1,0:T(8,128)(2,1)S(1)} reshape(bf16[16,12,3584]{2,1,0:T(8,128)(2,1)} %all-to-all-done.5) | data formatting | bytes 2752512 | tf_op jit(solution)/shard_map/reshape | solution.py:71
  179.8 2.5 %gather_fusion.1 = bf16[192,3584]{1,0:T(8,128)(2,1)} fusion(bf16[192,3584]{1,0:T(8,128)(2,1)S(1)} %reshape.238, s32[1024]{0:T(1024)S(1)} %pad_clamp_fusion), kind=kCustom, calls=%fused_computation.1 | custom fusion | bytes 2753280 | tf_op jit(solution)/shard_map/gather | solution.py:71
  182.3 1.9 fusion.20
  184.2 33.5 %all-to-all-done.2 = bf16[16,12,3584]{2,1,0:T(8,128)(2,1)S(1)} async-done(((bf16[16,12,3584]{2,1,0:T(8,128)(2,1)}), bf16[16,12,3584]{2,1,0:T(8,128)(2,1)S(1)}, u32[]{:S(2)}, u32[]{:S(2)}) %all-to-all-start.2) | async-done | bytes 1376288 | tf_op jit(solution)/shard_map/all_to_all | solution.py:70
  217.7 0.3 reshape.230
  218.1 0.0 copy-start.2
  218.1 1.7 gather_fusion
  219.8 0.0 copy-done.2
  219.8 0.5 fusion.24
  220.4 0.8 pad_maximum_fusion
  (21 shorter events, 0.4 us)
Async XLA Ops:
  5.3 13.9 %all-to-all-start.4 = ((bf16[16,2,168]{2,1,0:T(2,128)(2,1)}), bf16[16,2,168]{2,1,0:T(2,128)(2,1)S(1)}, u32[]{:S(2)}, u32[]{:S(2)}) async-start(bf16[16,2,168]{2,1,0:T(2,128)(2,1)} %reshape.300), calls=%async_computation.4 | async-start | bytes 32768 | tf_op jit(solution)/shard_map/all_to_all | solution.py:62
  19.1 9.9 %all-to-all-start.1 = ((bf16[16,2,168]{2,1,0:T(2,128)(2,1)}), bf16[16,2,168]{2,1,0:T(2,128)(2,1)S(1)}, u32[]{:S(2)}, u32[]{:S(2)}) async-start(bf16[16,2,168]{2,1,0:T(2,128)(2,1)} %reshape.302), calls=%async_computation.1 | async-start | bytes 32768 | tf_op jit(solution)/shard_map/all_to_all | solution.py:62
  29.0 47.3 %all-to-all-start.3 = ((bf16[16,12,3584]{2,1,0:T(8,128)(2,1)}), bf16[16,12,3584]{2,1,0:T(8,128)(2,1)}, u32[]{:S(2)}, u32[]{:S(2)}) async-start(bf16[16,12,3584]{2,1,0:T(8,128)(2,1)} %reshape.234), calls=%async_computation.3 | async-start | bytes 3670016 | tf_op jit(solution)/shard_map/all_to_all | solution.py:61
  44.0 37.2 %copy-start.1 = (f32[16,12,3584]{2,0,1:T(8,128)S(1)}, f32[16,12,3584]{2,0,1:T(8,128)}, u32[]{:S(2)}) copy-start(f32[16,12,3584]{2,0,1:T(8,128)} %mul.69) | copy-start | bytes 8257540
  76.3 47.2 %all-to-all-start = ((bf16[16,12,3584]{2,1,0:T(8,128)(2,1)}), bf16[16,12,3584]{2,1,0:T(8,128)(2,1)}, u32[]{:S(2)}, u32[]{:S(2)}) async-start(bf16[16,12,3584]{2,1,0:T(8,128)(2,1)} %reshape.226), calls=%async_computation | async-start | bytes 3670016 | tf_op jit(solution)/shard_map/all_to_all | solution.py:61
  103.3 25.0 %copy-start = (f32[16,12,3584]{2,0,1:T(8,128)S(1)}, f32[16,12,3584]{2,0,1:T(8,128)}, u32[]{:S(2)}) copy-start(f32[16,12,3584]{2,0,1:T(8,128)} %mul.61) | copy-start | bytes 8257540
  123.5 47.2 %all-to-all-start.5 = ((bf16[16,12,3584]{2,1,0:T(8,128)(2,1)}), bf16[16,12,3584]{2,1,0:T(8,128)(2,1)}, u32[]{:S(2)}, u32[]{:S(2)}) async-start(bf16[16,12,3584]{2,1,0:T(8,128)(2,1)} %reshape.237), calls=%async_computation.5 | async-start | bytes 3670016 | tf_op jit(solution)/shard_map/all_to_all | solution.py:70
  150.6 24.9 %copy-start.3 = (s32[2,24,8]{1,2,0:T(8,128)S(1)}, s32[2,24,8]{1,2,0:T(8,128)}, u32[]{:S(2)}) copy-start(s32[2,24,8]{1,2,0:T(8,128)} %param.10) | copy-start | bytes 4612
  170.7 47.1 %all-to-all-start.2 = ((bf16[16,12,3584]{2,1,0:T(8,128)(2,1)}), bf16[16,12,3584]{2,1,0:T(8,128)(2,1)S(1)}, u32[]{:S(2)}, u32[]{:S(2)}) async-start(bf16[16,12,3584]{2,1,0:T(8,128)(2,1)} %reshape.229), calls=%async_computation.2 | async-start | bytes 3670016 | tf_op jit(solution)/shard_map/all_to_all | solution.py:70
  218.1 1.7 copy-start.2
where the time goes:
time: 222 us; the launch traced here: 221 us
  waiting for transfers between devices  112 us (50%)
  local copies, waits for them, and re-layouts  36.8 us (17%)
  matrix products  30.4 us (14%)
  starting transfers between devices  30.2 us (14%)
  other arithmetic  11.7 us (5%)
    all_to_all x2, waiting for transfers between devices, shards(): lax.all_to_all(outputs, ('row', 'col'), split_axis=0, concat_axis=0, tile...  53.6 us
    all_to_all x2, waiting for transfers between devices, shards(): lax.all_to_all(send_rows, ('row', 'col'), split_axis=0, concat_axis=0, ti...  52.5 us
    dot_general x2, matrix products, expert_rows(): jnp.dot(hidden, down_matrix, preferred_element_type=jnp.float32)  17 us
    dot_general x2, matrix products, expert_rows(): gate = jnp.dot(inputs, gate_matrix, preferred_element_type=jnp.float32)  11.1 us
    all_to_all x2, starting transfers between devices, shards(): lax.all_to_all(send_scales, ('row', 'col'), split_axis=0, concat_axis=0,...  10.9 us
    all_to_all x2, starting transfers between devices, shards(): lax.all_to_all(send_rows, ('row', 'col'), split_axis=0, concat_axis=0, ti...  9.76 us
    all_to_all x2, starting transfers between devices, shards(): lax.all_to_all(outputs, ('row', 'col'), split_axis=0, concat_axis=0, tile...  9.55 us
    convert_element_type x2, other arithmetic, dequantize(): return scaled.reshape(values.shape).astype(jnp.bfloat16)  8.71 us
  transfers between devices with their start and end apart: 6, of which 6 were waited for; matrix products, arithmetic and copies ran while one was open for 32% of the time, Pallas kernels for 0%

commit v1 on v0

v1 whole, which is shorter than its diff:
```python
import functools

import jax
import jax.numpy as jnp
from jax import lax
from jax.experimental import pallas as pl
from jax.experimental.pallas import tpu as pltpu
from jax.sharding import PartitionSpec as P

MESH = pl.DeviceIdType.MESH
LANES = 128
TILE = 256


def kernel(ring, planar, tokens, half, payload, scales, ids, codes, wg_hbm, wu_hbm, wd_hbm, out, xa, xb, hid, y0, y1, s0, s1,
           i0, i1, r0, r1, wg, wu, wd, wsem, gsend, grecv, hsend, hrecv, rsend, rrecv, psend, precv):
    T, H = tokens, ring // 2
    width = 2 * half
    row, col = lax.axis_index("row"), lax.axis_index("col")
    expert = row * ring + col
    x, y, sib, inc, got = (xa, xb), (y0, y1), (s0, s1), (i0, i1), (r0, r1)

    def column(p):
        p = (p + ring) % ring
        if planar == 1:
            return p
        back = p // H
        return 2 * (p * (1 - back) + (ring - 1 - p) * back) + back

    if planar == 1:
        place = col
    else:
        place = (col // 2) * (1 - col % 2) + (ring - 1 - col // 2) * (col % 2)
    after, before = {"col": column(place + 1)}, {"col": column(place - 1)}
    other = {"row": 1 - row}
    onward = (after, before)
    homeward = (before, after)

    weights = [
        pltpu.make_async_copy(wg_hbm.at[0], wg, wsem.at[0]),
        pltpu.make_async_copy(wu_hbm.at[0], wu, wsem.at[1]),
        pltpu.make_async_copy(wd_hbm.at[0], wd, wsem.at[2]),
    ]
    for copy in weights:
        copy.start()

    barrier = pltpu.get_barrier_semaphore()
    for device in (after, before, other):
        pl.semaphore_signal(barrier, inc=1, device_id=device, device_id_type=MESH)

    lane = lax.broadcasted_iota(jnp.int32, (T, LANES), 1)
    dense = jnp.zeros((T, LANES), jnp.float32)
    for k in range(ids.shape[1]):
        dense += jnp.where(ids[:, k : k + 1] == lane, codes[:, k : k + 1], 0).astype(jnp.float32)
    xa[0, :T, half:] = dense.astype(jnp.bfloat16)
    for j in range(width // LANES):
        value = payload[:, j * LANES : (j + 1) * LANES].astype(jnp.float32) * scales[:, j : j + 1].astype(jnp.float32)
        side, at = divmod(j * LANES, half)
        x[side][0, :T, at : at + LANES] = value.astype(jnp.bfloat16)

    def single(d):
        return d == 0 or d == H

    def rows_in(d, way):
        return pl.ds(0 if single(d) else way * T, T)

    def rows_other(d, way):
        return pl.ds(T if single(d) else 2 * T + way * T, T)

    def gather_copy(d, way, sub):
        ch = way if sub == 0 else 1 - way
        return pltpu.make_async_remote_copy(
            x[ch].at[d - 1, rows_in(d - 1, way)], x[ch].at[d, rows_in(d, way)],
            gsend.at[d, way, sub], grecv.at[d, way, sub], device_id=onward[way], device_id_type=MESH)

    def share_copy(d, way, ch):
        return pltpu.make_async_remote_copy(
            x[ch].at[d, rows_in(d, way)], x[ch].at[d, rows_other(d, way)],
            hsend.at[d, way, ch], hrecv.at[d, way, ch], device_id=other, device_id_type=MESH)

    def reduce_copy(d, way, ch):
        return pltpu.make_async_remote_copy(
            y[ch].at[d, rows_in(d, way)], got[ch].at[d - 1, pl.ds(way * T, T)],
            rsend.at[d, way, ch], rrecv.at[d, way, ch], device_id=homeward[way], device_id_type=MESH)

    def pair_copy(d, ch):
        n = T if single(d) else 2 * T
        return pltpu.make_async_remote_copy(
            sib[ch].at[d, :n], inc[ch].at[d, :n],
            psend.at[d, ch], precv.at[d, ch], device_id=other, device_id_type=MESH)

    sends = []

    def start(copy):
        copy.start()
        sends.append(copy)

    def shares(d):
        if d == 0:
            return [(0, 0), (0, 1)]
        if d == H:
            return [(0, 0), (1, 1)]
        return [(way, ch) for way in (0, 1) for ch in (0, 1)]

    def arrive(d, sub):
        for way in (0, 1):
            gather_copy(d, way, sub).wait_recv()
            if d + 1 < H or (d + 1 == H and sub == 0):
                start(gather_copy(d + 1, way, sub))
            start(share_copy(d, way, way if sub == 0 else 1 - way))

    def gate_up(d):
        for way, ch in shares(d):
            share_copy(d, way, ch).wait_recv()
        m = 2 * T if single(d) else 4 * T
        lanes = lax.broadcasted_iota(jnp.int32, (m, LANES), 1)
        picked = jnp.where(lanes == expert, xa[d, :m, half:].astype(jnp.float32), 0.0)
        code = jnp.sum(picked, axis=1, keepdims=True)

        def step(i, carry):
            c = pl.ds(pl.multiple_of(i * TILE, TILE), TILE)
            left, right = xa[d, :m, :half], xb[d, :m, :]
            g = jnp.dot(left, wg[:half, c], preferred_element_type=jnp.float32)
            g += jnp.dot(right, wg[half:, c], preferred_element_type=jnp.float32)
            u = jnp.dot(left, wu[:half, c], preferred_element_type=jnp.float32)
            u += jnp.dot(right, wu[half:, c], preferred_element_type=jnp.float32)
            hid[:m, c] = (g / (1.0 + jnp.exp(-g)) * u * code).astype(jnp.bfloat16)
            return carry

        lax.fori_loop(0, wg.shape[1] // TILE, step, 0)

    def down(d, ch):
        m = 2 * T if single(d) else 4 * T
        n = m // 2

        def step(i, carry):
            c = pl.ds(pl.multiple_of(i * TILE, TILE), TILE)
            w = pl.ds(pl.multiple_of(ch * half + i * TILE, TILE), TILE)
            o = jnp.dot(hid[:m], wd[:, w], preferred_element_type=jnp.float32).astype(jnp.bfloat16)
            y[ch][d, :n, c] = o[:n]
            sib[ch][d, :n, c] = o[n:]
            return carry

        lax.fori_loop(0, half // TILE, step, 0)
        start(pair_copy(d, ch))

    def downs(d):
        down(d, 0)
        down(d, 1)

    paired = set()

    def item(d, sub):
        for way in (0, 1):
            ch = way if sub == 0 else 1 - way
            if (d, ch) not in paired:
                pair_copy(d, ch).wait_recv()
                paired.add((d, ch))
            at = rows_in(d, way)
            total = y[ch][d, at, :].astype(jnp.float32) + inc[ch][d, at, :].astype(jnp.float32)
            if d + 1 < H or (d + 1 == H and sub == 0):
                reduce_copy(d + 1, way, ch).wait_recv()
                total += got[ch][d, pl.ds(way * T, T), :].astype(jnp.float32)
            y[ch][d, at, :] = total.astype(jnp.bfloat16)
            start(reduce_copy(d, way, ch))

    pl.semaphore_wait(barrier, 3)
    for way in (0, 1):
        start(gather_copy(1, way, 0))
    for ch in (0, 1):
        start(share_copy(0, 0, ch))
    for way in (0, 1):
        start(gather_copy(1, way, 1))

    arrive(1, 0)
    arrive(1, 1)
    weights[0].wait()
    weights[1].wait()
    gate_up(0)
    arrive(2, 0)
    weights[2].wait()
    downs(0)
    gate_up(1)
    if H > 2:
        arrive(2, 1)
    downs(1)
    for d in range(2, H):
        if d + 1 < H:
            arrive(d + 1, 0)
            gate_up(d)
            arrive(d + 1, 1)
            downs(d)
        else:
            gate_up(d)
            arrive(H, 0)
            downs(d)
    item(H - 1, 1)
    gate_up(H)
    downs(H)
    for d in range(H, 1, -1):
        item(d, 0)
        if d - 2 >= 1:
            item(d - 2, 1)
    item(1, 0)

    total_code = jnp.sum(codes[...].astype(jnp.float32), axis=1, keepdims=True)
    for ch in (0, 1):
        pair_copy(0, ch).wait_recv()
    for ch in (0, 1):
        total = y[ch][0, :T, :].astype(jnp.float32) + inc[ch][0, :T, :].astype(jnp.float32)
        for way in (1 - ch, ch):
            reduce_copy(1, way, ch).wait_recv()
            total += got[ch][0, pl.ds(way * T, T), :].astype(jnp.float32)
        out[:, ch * half : (ch + 1) * half] = (total / total_code).astype(jnp.bfloat16)
    for copy in sends:
        copy.wait_send()


def shards(ring, planar, payload, block_scales, expert_ids, gate_codes, w_gate, w_up, w_down):
    micro, local, width = payload.shape
    tokens, half, H = micro * local, width // 2, ring // 2
    hidden = w_gate.shape[2]
    flat = [a.reshape(tokens, a.shape[2]) for a in (payload, block_scales, expert_ids, gate_codes)]
    vmem, hbm = pl.BlockSpec(memory_space=pltpu.VMEM), pl.BlockSpec(memory_space=pl.ANY)
    bf16, dma = jnp.bfloat16, pltpu.SemaphoreType.DMA
    mixed = pl.pallas_call(
        functools.partial(kernel, ring, planar, tokens, half),
        out_shape=jax.ShapeDtypeStruct((tokens, width), bf16),
        in_specs=[vmem] * 4 + [hbm] * 3,
        out_specs=vmem,
        scratch_shapes=[
            pltpu.VMEM((H + 1, 4 * tokens, half + LANES), bf16),
            pltpu.VMEM((H + 1, 4 * tokens, half), bf16),
            pltpu.VMEM((4 * tokens, hidden), bf16),
            *[pltpu.VMEM((H + 1, 2 * tokens, half), bf16)] * 6,
            *[pltpu.VMEM((H, 2 * tokens, half), bf16)] * 2,
            pltpu.VMEM((width, hidden), bf16),
            pltpu.VMEM((width, hidden), bf16),
            pltpu.VMEM((hidden, width), bf16),
            dma((3,)),
            *[dma((H + 1, 2, 2))] * 6,
            *[dma((H + 1, 2))] * 2,
        ],
        compiler_params=pltpu.CompilerParams(
            collective_id=0, has_side_effects=True, vmem_limit_bytes=62 * 1024 * 1024
        ),
    )(*flat, w_gate, w_up, w_down)
    return mixed.reshape(micro, local, width)


def solution(mesh):
    ring = mesh.shape["col"]
    planar = max(1, 4 // mesh.shape["groups"])
    spread = P(None, ("groups", "row", "col"), None)
    placed = P(("row", "col"), None, None)
    return jax.shard_map(
        functools.partial(shards, ring, planar),
        mesh=mesh,
        in_specs=(spread,) * 4 + (placed,) * 3,
        out_specs=spread,
        check_vma=False,
    )
```

time: 222 us -> 87.2 us (0.39)
  waiting for transfers between devices: 112 us -> 0 us
  Pallas kernels: 0 us -> 82.5 us
  local copies, waits for them, and re-layouts: 36.8 us -> 4.5 us
  matrix products: 30.4 us -> 0 us
  starting transfers between devices: 30.2 us -> 0 us
  other arithmetic: 11.7 us -> 0 us
    all_to_all x6 -> x0, waiting for transfers between devices: 112 us -> none  [the longest x2 53.6 us: shards(): lax.all_to_all(outputs, ('row', 'col'), split_axis=0, concat_axis=0, tile...]
    pallas_call x0 -> x1, Pallas kernels: none -> 82.5 us  [shards(): pl.pallas_call(functools.partial(kernel, ring, planar, tokens, half), out...]
    dot_general x6 -> x0, matrix products: 30.4 us -> none  [the longest x2 17 us: expert_rows(): jnp.dot(hidden, down_matrix, preferred_element_type=jnp.float32)]
    all_to_all x6 -> x0, starting transfers between devices: 30.2 us -> none  [the longest x2 10.9 us: shards(): lax.all_to_all(send_scales, ('row', 'col'), split_axis=0, concat_axis=0,...]
    reshape x12 -> x0, local copies, waits for them, and re-layouts: 13.5 us -> none  [the longest x2 4.72 us: shards(): dequant.reshape(outer * inner, width)]
    convert_element_type x4 -> x0, other arithmetic: 8.73 us -> none  [the longest x2 8.71 us: dequantize(): return scaled.reshape(values.shape).astype(jnp.bfloat16)]
    scatter x4 -> x0, local copies, waits for them, and re-layouts: 7.77 us -> none  [the longest x2 5.71 us: shards(): jnp.zeros((slot_total, width), jnp.bfloat16).at[position].set(spread_rows)]
    mul x4 -> x0, local copies, waits for them, and re-layouts: 5.36 us -> none  [dequantize(): scaled = shaped * block_scales.astype(jnp.float32)[..., None]]
  transfers between devices with their start and end apart: 6 -> 0, of which waited for: 6 -> 0; matrix products, arithmetic and copies ran while one was open for 32% -> 0% of each run, Pallas kernels for 0% -> 0%
where the time goes in v1:
time: 87.2 us; the launch traced here: 87 us
  Pallas kernels  82.5 us (95%)
  local copies, waits for them, and re-layouts  4.5 us (5%)
    pallas_call x1, Pallas kernels, shards(): pl.pallas_call(functools.partial(kernel, ring, planar, tokens, half), out...  82.5 us
    unnamed x3, local copies, waits for them, and re-layouts  4.5 us

profile of v1, /device:TPU:0, one launch (start us, length us, event | category | flops | bytes accessed | tf_op | source)
XLA Modules:
  0.0 87.0 jit_solution(2586175154528735728)
XLA Ops:
  0.0 1.4 %copy.8 = s32[2,24,8]{2,1,0:T(8,128)} copy(s32[2,24,8]{1,2,0:T(8,128)} %param.9) | data formatting | bytes 3072 | tf_op args[2]
  1.4 1.4 %copy.9 = s32[2,24,8]{2,1,0:T(8,128)} copy(s32[2,24,8]{1,2,0:T(8,128)} %param.10) | data formatting | bytes 3072 | tf_op args[3]
  2.8 82.5 %shard_map.73 = bf16[48,3584]{1,0:T(8,128)(2,1)} custom-call(bf16[48,3584]{1,0:T(8,128)(2,1)} %bitcast.6, bf16[48,28]{1,0:T(8,128)(2,1)} %bitcast.9, s32[48,8]{1,0:T(8,128)} %bitcast.7, s32[48,8]{1,0:T(8,128)} %bitcast.8, bf16[1,3584,1024]{2,1,0:T(8,128)(2,1)} %wg_hbm.1, bf16[1,3584,1024]{2,1,0:T(8,128)(2,1)} %wu_hbm.1, bf16[1,1024,3584]{2,1,0:T(8,128)(2,1)} %wd_hbm.1), custom_call_target="tpu_custom_call" | custom-call | tf_op jit(solution)/shard_map/pallas_call | solution.py:226
  85.2 1.7 %copy.11 = bf16[2,24,3584]{2,1,0:T(8,128)(2,1)} copy(bf16[2,24,3584]{2,1,0:T(8,128)(2,1)} %bitcast.5) | data formatting | bytes 688128

commit v2 on v1

--- a/solution.py
+++ b/solution.py
@@ -9,7 +9,7 @@
 
 MESH = pl.DeviceIdType.MESH
 LANES = 128
-TILE = 256
+TILE = 512
 
 
 def kernel(ring, planar, tokens, half, payload, scales, ids, codes, wg_hbm, wu_hbm, wd_hbm, out, xa, xb, hid, y0, y1, s0, s1,
@@ -48,15 +48,24 @@
     for device in (after, before, other):
         pl.semaphore_signal(barrier, inc=1, device_id=device, device_id_type=MESH)
 
-    lane = lax.broadcasted_iota(jnp.int32, (T, LANES), 1)
-    dense = jnp.zeros((T, LANES), jnp.float32)
-    for k in range(ids.shape[1]):
-        dense += jnp.where(ids[:, k : k + 1] == lane, codes[:, k : k + 1], 0).astype(jnp.float32)
+    local = T // ids.shape[0]
+    lane = lax.broadcasted_iota(jnp.int32, (local, LANES), 1)
+    parts, sums = [], []
+    for micro in range(ids.shape[0]):
+        named, code = jnp.swapaxes(ids[micro], 0, 1), jnp.swapaxes(codes[micro], 0, 1)
+        dense = jnp.zeros((local, LANES), jnp.float32)
+        for k in range(named.shape[1]):
+            dense += jnp.where(named[:, k : k + 1] == lane, code[:, k : k + 1], 0).astype(jnp.float32)
+        parts.append(dense)
+    dense = jnp.concatenate(parts, axis=0)
+    inverse = 1.0 / jnp.sum(dense, axis=1, keepdims=True)
     xa[0, :T, half:] = dense.astype(jnp.bfloat16)
-    for j in range(width // LANES):
-        value = payload[:, j * LANES : (j + 1) * LANES].astype(jnp.float32) * scales[:, j : j + 1].astype(jnp.float32)
-        side, at = divmod(j * LANES, half)
-        x[side][0, :T, at : at + LANES] = value.astype(jnp.bfloat16)
+
+    def dequantize(side):
+        for j in range(half // LANES):
+            at, block = side * half + j * LANES, side * (half // LANES) + j
+            value = payload[:, at : at + LANES].astype(jnp.float32) * scales[:, block : block + 1].astype(jnp.float32)
+            x[side][0, :T, j * LANES : (j + 1) * LANES] = value.astype(jnp.bfloat16)
 
     def single(d):
         return d == 0 or d == H
@@ -133,15 +142,10 @@
         m = 2 * T if single(d) else 4 * T
         n = m // 2
 
-        def step(i, carry):
-            c = pl.ds(pl.multiple_of(i * TILE, TILE), TILE)
-            w = pl.ds(pl.multiple_of(ch * half + i * TILE, TILE), TILE)
-            o = jnp.dot(hid[:m], wd[:, w], preferred_element_type=jnp.float32).astype(jnp.bfloat16)
-            y[ch][d, :n, c] = o[:n]
-            sib[ch][d, :n, c] = o[n:]
-            return carry
-
-        lax.fori_loop(0, half // TILE, step, 0)
+        w = wd[:, ch * half : (ch + 1) * half]
+        o = jnp.dot(hid[:m], w, preferred_element_type=jnp.float32).astype(jnp.bfloat16)
+        y[ch][d, :n, :] = o[:n]
+        sib[ch][d, :n, :] = o[n:]
         start(pair_copy(d, ch))
 
     def downs(d):
@@ -164,8 +168,10 @@
             y[ch][d, at, :] = total.astype(jnp.bfloat16)
             start(reduce_copy(d, way, ch))
 
-    pl.semaphore_wait(barrier, 3)
     for way in (0, 1):
+        dequantize(way)
+        if way == 0:
+            pl.semaphore_wait(barrier, 3)
         start(gather_copy(1, way, 0))
     for ch in (0, 1):
         start(share_copy(0, 0, ch))
@@ -203,7 +209,6 @@
             item(d - 2, 1)
     item(1, 0)
 
-    total_code = jnp.sum(codes[...].astype(jnp.float32), axis=1, keepdims=True)
     for ch in (0, 1):
         pair_copy(0, ch).wait_recv()
     for ch in (0, 1):
@@ -211,7 +216,7 @@
         for way in (1 - ch, ch):
             reduce_copy(1, way, ch).wait_recv()
             total += got[ch][0, pl.ds(way * T, T), :].astype(jnp.float32)
-        out[:, ch * half : (ch + 1) * half] = (total / total_code).astype(jnp.bfloat16)
+        out[:, ch * half : (ch + 1) * half] = (total * inverse).astype(jnp.bfloat16)
     for copy in sends:
         copy.wait_send()
 
@@ -220,7 +225,8 @@
     micro, local, width = payload.shape
     tokens, half, H = micro * local, width // 2, ring // 2
     hidden = w_gate.shape[2]
-    flat = [a.reshape(tokens, a.shape[2]) for a in (payload, block_scales, expert_ids, gate_codes)]
+    flat = [a.reshape(tokens, a.shape[2]) for a in (payload, block_scales)]
+    flat += [jnp.swapaxes(a, 1, 2) for a in (expert_ids, gate_codes)]
     vmem, hbm = pl.BlockSpec(memory_space=pltpu.VMEM), pl.BlockSpec(memory_space=pl.ANY)
     bf16, dma = jnp.bfloat16, pltpu.SemaphoreType.DMA
     mixed = pl.pallas_call(

time: 87.2 us -> 74.3 us (0.85)
  Pallas kernels: 82.5 us -> 72.4 us
  local copies, waits for them, and re-layouts: 4.5 us -> 1.73 us
    pallas_call x1, Pallas kernels: 82.5 us -> 72.4 us  [shards(): pl.pallas_call(functools.partial(kernel, ring, planar, tokens, half), out...]
    unnamed x3 -> x1, local copies, waits for them, and re-layouts: 4.5 us -> 1.73 us
where the time goes in v2:
time: 74.3 us; the launch traced here: 74.1 us
  Pallas kernels  72.4 us (97%)
  local copies, waits for them, and re-layouts  1.73 us (2%)
    pallas_call x1, Pallas kernels, shards(): pl.pallas_call(functools.partial(kernel, ring, planar, tokens, half), out...  72.4 us
    unnamed x1, local copies, waits for them, and re-layouts  1.73 us

profile of v2, /device:TPU:0, one launch (start us, length us, event | category | flops | bytes accessed | tf_op | source)
XLA Modules:
  0.0 74.1 jit_solution(16383524908253767247)
XLA Ops:
  0.0 72.4 %shard_map.73 = bf16[48,3584]{1,0:T(8,128)(2,1)} custom-call(bf16[48,3584]{1,0:T(8,128)(2,1)} %bitcast.6, bf16[48,28]{1,0:T(8,128)(2,1)} %bitcast.7, s32[2,8,24]{2,1,0:T(8,128)} %bitcast.8, s32[2,8,24]{2,1,0:T(8,128)} %bitcast.9, bf16[1,3584,1024]{2,1,0:T(8,128)(2,1)} %wg_hbm.1, bf16[1,3584,1024]{2,1,0:T(8,128)(2,1)} %wu_hbm.1, bf16[1,1024,3584]{2,1,0:T(8,128)(2,1)} %wd_hbm.1), custom_call_target="tpu_custom_call" | custom-call | tf_op jit(solution)/shard_map/pallas_call | solution.py:232
  72.4 1.7 %copy.9 = bf16[2,24,3584]{2,1,0:T(8,128)(2,1)} copy(bf16[2,24,3584]{2,1,0:T(8,128)(2,1)} %bitcast.5) | data formatting | bytes 688128

commit v3 on v2

--- a/solution.py
+++ b/solution.py
@@ -133,7 +133,7 @@
             g += jnp.dot(right, wg[half:, c], preferred_element_type=jnp.float32)
             u = jnp.dot(left, wu[:half, c], preferred_element_type=jnp.float32)
             u += jnp.dot(right, wu[half:, c], preferred_element_type=jnp.float32)
-            hid[:m, c] = (g / (1.0 + jnp.exp(-g)) * u * code).astype(jnp.bfloat16)
+            hid[d % 3, :m, c] = (g / (1.0 + jnp.exp(-g)) * u * code).astype(jnp.bfloat16)
             return carry
 
         lax.fori_loop(0, wg.shape[1] // TILE, step, 0)
@@ -143,7 +143,7 @@
         n = m // 2
 
         w = wd[:, ch * half : (ch + 1) * half]
-        o = jnp.dot(hid[:m], w, preferred_element_type=jnp.float32).astype(jnp.bfloat16)
+        o = jnp.dot(hid[d % 3, :m], w, preferred_element_type=jnp.float32).astype(jnp.bfloat16)
         y[ch][d, :n, :] = o[:n]
         sib[ch][d, :n, :] = o[n:]
         start(pair_copy(d, ch))
@@ -195,7 +195,8 @@
             arrive(d + 1, 0)
             gate_up(d)
             arrive(d + 1, 1)
-            downs(d)
+            if d < H - 2:
+                downs(d)
         else:
             gate_up(d)
             arrive(H, 0)
@@ -205,6 +206,8 @@
     downs(H)
     for d in range(H, 1, -1):
         item(d, 0)
+        if d == H and H >= 4:
+            downs(H - 2)
         if d - 2 >= 1:
             item(d - 2, 1)
     item(1, 0)
@@ -237,7 +240,7 @@
         scratch_shapes=[
             pltpu.VMEM((H + 1, 4 * tokens, half + LANES), bf16),
             pltpu.VMEM((H + 1, 4 * tokens, half), bf16),
-            pltpu.VMEM((4 * tokens, hidden), bf16),
+            pltpu.VMEM((3, 4 * tokens, hidden), bf16),
             *[pltpu.VMEM((H + 1, 2 * tokens, half), bf16)] * 6,
             *[pltpu.VMEM((H, 2 * tokens, half), bf16)] * 2,
             pltpu.VMEM((width, hidden), bf16),

time: 74.3 us -> 73.6 us (level)
  no operation moved by 1% of the time
where the time goes in v3:
time: 73.6 us; the launch traced here: 73.5 us
  Pallas kernels  71.7 us (97%)
  local copies, waits for them, and re-layouts  1.73 us (2%)
    pallas_call x1, Pallas kernels, shards(): pl.pallas_call(functools.partial(kernel, ring, planar, tokens, half), out...  71.7 us
    unnamed x1, local copies, waits for them, and re-layouts  1.73 us

profile of v3, /device:TPU:0, one launch (start us, length us, event | category | flops | bytes accessed | tf_op | source)
XLA Modules:
  0.0 73.5 jit_solution(4305803859746030243)
XLA Ops:
  0.0 71.7 %shard_map.73 = bf16[48,3584]{1,0:T(8,128)(2,1)} custom-call(bf16[48,3584]{1,0:T(8,128)(2,1)} %bitcast.6, bf16[48,28]{1,0:T(8,128)(2,1)} %bitcast.7, s32[2,8,24]{2,1,0:T(8,128)} %bitcast.8, s32[2,8,24]{2,1,0:T(8,128)} %bitcast.9, bf16[1,3584,1024]{2,1,0:T(8,128)(2,1)} %wg_hbm.1, bf16[1,3584,1024]{2,1,0:T(8,128)(2,1)} %wu_hbm.1, bf16[1,1024,3584]{2,1,0:T(8,128)(2,1)} %wd_hbm.1), custom_call_target="tpu_custom_call" | custom-call | tf_op jit(solution)/shard_map/pallas_call | solution.py:235
  71.7 1.7 %copy.9 = bf16[2,24,3584]{2,1,0:T(8,128)(2,1)} copy(bf16[2,24,3584]{2,1,0:T(8,128)(2,1)} %bitcast.5) | data formatting | bytes 688128
